TPU v7x, 32 devices: a whole 2x2x4 slice. The times are simulated.
32 devices in a mesh: member: 4 (over z), cell: 8 (over y, x, core).
Axes of the slice: x: 2, y: 2, z: 4, core: 2. Of those that a mesh axis runs over, the one named last changes fastest.
Arguments:
- prior: float32 [64, 131072], P('member', 'cell')
- samples: float32 [64, 131072], P('member', 'cell')
- noise: float32 [2, 64, 131072], P(None, 'member', 'cell'), may hold values from -6 to 6
- obs_cells: int32 [2, 16384], P(None, 'cell'), may hold values from 0 to 131071, as said below
- obs_values: float32 [2, 16384], P(None, 'cell'), may hold values from -6 to 6
- seismic_mask: int32 [2, 1024], P(None, 'cell'), may hold values 0 or 1
Outputs:
- analysis: float32 [64, 131072], P('member', 'cell')
Inputs may be any that keep to these rules, and one draw needn't show every extreme that they name: obs_cells[s, o] lies in cells k * 16384 to (k + 1) * 16384 - 1 where k = o // 2048; cells may repeat.
All inputs are finite; a program needn't handle non-finite values. No bound on the sum of `seismic_mask` on one device may be relied on, other than what follows from the above.
Results may differ from a plain program's by a relative error of at most 0.0003.
Values sent between devices are 32-bit elements; how exact they have to be, the bound alone decides.
A program may use at most 64 MiB of HBM per device.

v0:
```python
import math

import jax
import jax.numpy as jnp
from jax import lax
from jax.sharding import PartitionSpec as P

STEPS = 2


def advance(state, fresh, prior_slab, prior_part, precision_slab, target_slab, step, ncell):
    time_now = 0.6 - 0.1 * step
    alpha = 1.0 - 0.95 * time_now
    drift = -0.95 / alpha
    diffusion = 1.0 - 2.0 * drift * time_now
    cross_part = lax.dot_general(
        state,
        prior_slab,
        (((1,), (1,)), ((), ())),
        precision=lax.Precision.HIGHEST,
        preferred_element_type=jnp.float32,
    )
    cross, prior_sq = lax.psum((cross_part, prior_part), ("member", "cell"))
    dist = alpha * alpha * prior_sq[None, :] - 2.0 * alpha * cross
    weights = jax.nn.softmax(-dist / (2.0 * time_now * math.sqrt(ncell)), axis=1)
    mean = jnp.dot(
        weights, prior_slab, precision=lax.Precision.HIGHEST, preferred_element_type=jnp.float32
    )
    score = (alpha * mean - state) / time_now - (1.0 - time_now) * (
        precision_slab[None, :] * state - target_slab[None, :]
    )
    return state - 0.1 * (drift * state - diffusion * score) + math.sqrt(0.1 * diffusion) * fresh


def per_device(prior, samples, noise, obs_cells, obs_values, seismic_mask):
    cells = prior.shape[1]
    groups = lax.axis_size("member")
    width = cells // groups
    ncell = cells * lax.axis_size("cell")
    shard = lax.axis_index("cell")
    member_pos = lax.axis_index("member")
    local = obs_cells - shard * cells
    precision_field = jnp.zeros((cells,), jnp.float32)
    target_field = jnp.zeros((cells,), jnp.float32)
    for survey in range(obs_cells.shape[0]):
        where = local[survey]
        flags = seismic_mask[survey].astype(jnp.float32)
        weight = flags[where // 128]
        precision_field = precision_field.at[where].add(weight)
        target_field = target_field.at[where].add(weight * obs_values[survey])
    precision_slab = lax.dynamic_slice_in_dim(precision_field, member_pos * width, width)
    target_slab = lax.dynamic_slice_in_dim(target_field, member_pos * width, width)
    prior_slab = lax.all_to_all(prior, "member", split_axis=1, concat_axis=0, tiled=True)
    prior_part = jnp.sum(prior_slab * prior_slab, axis=1)
    state = samples
    for step in range(STEPS):
        slab, fresh = (
            lax.all_to_all(state, "member", split_axis=1, concat_axis=0, tiled=True),
            lax.all_to_all(noise[step], "member", split_axis=1, concat_axis=0, tiled=True),
        )
        slab = advance(
            slab, fresh, prior_slab, prior_part, precision_slab, target_slab, step, ncell
        )
        state = lax.all_to_all(slab, "member", split_axis=0, concat_axis=1, tiled=True)
    return state


def solution(mesh):
    in_specs = (
        P("member", "cell"),
        P("member", "cell"),
        P(None, "member", "cell"),
        P(None, "cell"),
        P(None, "cell"),
        P(None, "cell"),
    )
    out_specs = P("member", "cell")
    return jax.shard_map(
        per_device, mesh=mesh, in_specs=in_specs, out_specs=out_specs, check_vma=False
    )
```

profile of v0, /device:TPU:0, one launch (start us, length us, event | category | flops | bytes accessed | tf_op | source)
XLA Modules:
  0.0 342.8 jit_solution(4444424029722977596)
XLA Ops:
  0.0 0.0 copy-start
  0.0 2.4 copy.34
  2.4 6.3 %all-to-all-start = ((f32[16,4,4096]{2,0,1:T(8,128)}), f32[16,4,4096]{2,0,1:T(8,128)S(1)}, u32[]{:S(2)}, u32[]{:S(2)}) async-start(f32[16,4,4096]{2,0,1:T(8,128)} %bitcast.59), calls=%async_computation | async-start | bytes 2097152 | tf_op jit(solution)/shard_map/all_to_all | solution.py:58
  8.7 0.0 copy-done
  8.7 1.1 copy.33
  9.7 24.7 %all-to-all-done = f32[16,4,4096]{2,0,1:T(8,128)S(1)} async-done(((f32[16,4,4096]{2,0,1:T(8,128)}), f32[16,4,4096]{2,0,1:T(8,128)S(1)}, u32[]{:S(2)}, u32[]{:S(2)}) %all-to-all-start) | async-done | bytes 1048608 | tf_op jit(solution)/shard_map/all_to_all | solution.py:58
  34.4 3.5 %all-to-all-start.1 = ((f32[16,4,4096]{2,0,1:T(8,128)}), f32[16,4,4096]{2,0,1:T(8,128)S(1)}, u32[]{:S(2)}, u32[]{:S(2)}) async-start(f32[16,4,4096]{2,0,1:T(8,128)} %bitcast.58), calls=%async_computation.1 | async-start | bytes 2097152 | tf_op jit(solution)/shard_map/all_to_all | solution.py:53
  37.9 3.1 fusion.41
  41.0 0.0 copy-start.1
  41.0 1.9 all_to_all.94
  42.9 1.6 copy.24
  44.5 0.0 copy-done.1
  44.6 18.6 %all-to-all-done.1 = f32[16,4,4096]{2,0,1:T(8,128)S(1)} async-done(((f32[16,4,4096]{2,0,1:T(8,128)}), f32[16,4,4096]{2,0,1:T(8,128)S(1)}, u32[]{:S(2)}, u32[]{:S(2)}) %all-to-all-start.1) | async-done | bytes 1048608 | tf_op jit(solution)/shard_map/all_to_all | solution.py:53
  63.1 3.5 %all-to-all-start.2 = ((f32[16,4,4096]{2,0,1:T(8,128)}), f32[16,4,4096]{2,0,1:T(8,128)S(1)}, u32[]{:S(2)}, u32[]{:S(2)}) async-start(f32[16,4,4096]{2,0,1:T(8,128)} %copy.24), calls=%async_computation.2 | async-start | bytes 2097152 | tf_op jit(solution)/shard_map/all_to_all | solution.py:59
  66.6 0.1 compare_select_fusion
  66.8 0.0 copy-start.3
  66.8 2.9 all_to_all.102
  69.7 2.9 copy.25
  72.5 0.0 copy-done.3
  72.6 0.0 copy-start.2
  72.6 12.6 %gather_fusion = f32[2048]{0:T(1024)S(1)} fusion(f32[128]{0:T(128)S(1)} %get-tuple-element.16, s32[2048]{0:T(1024)S(1)} %broadcast_clamp_fusion.1), kind=kCustom, calls=%fused_computation | custom fusion | bytes 24576 | tf_op jit(solution)/shard_map/gather | solution.py:48
  85.2 0.0 copy-done.2
  85.2 11.3 %scatter_custom_fusion = f32[16384]{0:T(1024)S(1)} fusion(s32[2048]{0:T(1024)S(1)} %bitcast.82, f32[2048]{0:T(1024)S(1)} %gather_fusion, f32[]{:T(128)} %constant.32.clone.1), kind=kCustom, calls=%fused_computation.37 | custom fusion | flops 2048 | bytes 65540 | tf_op jit(solution)/shard_map/scatter-add | solution.py:49
  96.5 11.3 %scatter_custom_fusion.2 = f32[16384]{0:T(1024)S(1)} fusion(s32[2048]{0:T(1024)S(1)} %bitcast.83, f32[2048]{0:T(1024)S(1)} %mul.145, f32[]{:T(128)} %constant.32.clone.1), kind=kCustom, calls=%fused_computation.35 | custom fusion | flops 2048 | bytes 65540 | tf_op jit(solution)/shard_map/scatter-add | solution.py:50
  107.8 12.6 %gather_fusion.1 = f32[2048]{0:T(1024)S(1)} fusion(f32[128]{0:T(128)S(1)} %get-tuple-element.15, s32[2048]{0:T(1024)S(1)} %broadcast_clamp_fusion), kind=kCustom, calls=%fused_computation.1 | custom fusion | bytes 24576 | tf_op jit(solution)/shard_map/gather | solution.py:48
  120.5 11.6 %scatter_fusion = f32[16384]{0:T(1024)S(1)} fusion(f32[16384]{0:T(1024)S(1)} %scatter_custom_fusion, s32[2048]{0:T(1024)S(1)} %bitcast.76, f32[2048]{0:T(1024)S(1)} %gather_fusion.1), kind=kCustom, calls=%fused_computation.3 | custom fusion | flops 2048 | bytes 32768 | tf_op jit(solution)/shard_map/scatter-add | solution.py:49
  132.0 11.6 %scatter_fusion.1 = f32[16384]{0:T(1024)S(1)} fusion(f32[16384]{0:T(1024)S(1)} %scatter_custom_fusion.2, s32[2048]{0:T(1024)S(1)} %bitcast.77, f32[2048]{0:T(1024)S(1)} %mul.146), kind=kCustom, calls=%fused_computation.5 | custom fusion | flops 2048 | bytes 32768 | tf_op jit(solution)/shard_map/scatter-add | solution.py:50
  143.6 0.1 fusion.16
  143.8 0.1 reduce_sum.30
  143.9 1.0 fusion.43
  144.9 41.1 %all-reduce = (f32[64,64]{1,0:T(8,128)S(1)}, f32[64]{0:T(128)S(1)}) all-reduce(f32[64,64]{1,0:T(8,128)S(1)} %fusion.43, f32[64]{0:T(128)S(1)} %reduce_sum.30), channel_id=1, replica_groups=mesh['member'=4,'cell'=8] {'member','cell'}, use_global_device_ids=true, to_apply=%region_2.3 | all-reduce | flops 4160 | bytes 33280 | tf_op jit(solution)/shard_map/psum | solution.py:23
  186.0 0.0 all-to-all-done.2
  186.0 4.4 %all-to-all-start.5 = ((f32[16,4,4096]{2,0,1:T(8,128)}), f32[16,4,4096]{2,0,1:T(8,128)}, u32[]{:S(2)}, u32[]{:S(2)}) async-start(f32[16,4,4096]{2,0,1:T(8,128)} %copy.25), calls=%async_computation.5 | async-start | bytes 2097152 | tf_op jit(solution)/shard_map/all_to_all | solution.py:59
  190.5 0.1 fusion.25
  190.6 0.2 fusion.23
  190.8 0.1 broadcast_multiply_fusion.1
  190.9 1.5 fusion.8
  192.3 23.2 %all-to-all-done.5 = f32[16,4,4096]{2,0,1:T(8,128)} async-done(((f32[16,4,4096]{2,0,1:T(8,128)}), f32[16,4,4096]{2,0,1:T(8,128)}, u32[]{:S(2)}, u32[]{:S(2)}) %all-to-all-start.5) | async-done | bytes 1048608 | tf_op jit(solution)/shard_map/all_to_all | solution.py:59
  215.6 28.4 %all_to_all.115 = f32[4,16,4096]{2,1,0:T(8,128)} all-to-all(f32[4,16,4096]{2,1,0:T(8,128)S(1)} %bitcast.69), channel_id=1, replica_groups=mesh['member'=4,'cell'=8] {'member'}, dimensions={0} | all-to-all | bytes 2097152 | tf_op jit(solution)/shard_map/all_to_all | solution.py:64
  243.9 3.5 %all-to-all-start.4 = ((f32[16,4,4096]{2,0,1:T(8,128)}), f32[16,4,4096]{2,0,1:T(8,128)S(1)}, u32[]{:S(2)}, u32[]{:S(2)}) async-start(f32[16,4,4096]{2,0,1:T(8,128)} %bitcast.72), calls=%async_computation.4 | async-start | bytes 2097152 | tf_op jit(solution)/shard_map/all_to_all | solution.py:58
  247.4 1.3 broadcast_multiply_fusion
  248.8 23.4 %all-to-all-done.4 = f32[16,4,4096]{2,0,1:T(8,128)S(1)} async-done(((f32[16,4,4096]{2,0,1:T(8,128)}), f32[16,4,4096]{2,0,1:T(8,128)S(1)}, u32[]{:S(2)}, u32[]{:S(2)}) %all-to-all-start.4) | async-done | bytes 1048608 | tf_op jit(solution)/shard_map/all_to_all | solution.py:58
  272.2 1.0 fusion.44
  273.2 37.8 %psum.26 = f32[64,64]{1,0:T(8,128)S(1)} all-reduce(f32[64,64]{1,0:T(8,128)S(1)} %fusion.44), channel_id=1, replica_groups=mesh['member'=4,'cell'=8] {'member','cell'}, use_global_device_ids=true, to_apply=%region_9.10 | all-reduce | flops 4096 | bytes 32768 | tf_op jit(solution)/shard_map/psum | solution.py:23
  311.0 0.1 fusion.26
  311.1 0.2 fusion.24
  311.3 1.5 fusion.15
  312.8 29.0 %all_to_all.116 = f32[4,16,4096]{2,1,0:T(8,128)S(1)} all-to-all(f32[4,16,4096]{2,1,0:T(8,128)S(1)} %bitcast.70), channel_id=1, replica_groups=mesh['member'=4,'cell'=8] {'member'}, dimensions={0} | all-to-all | bytes 2097152 | tf_op jit(solution)/shard_map/all_to_all | solution.py:64
  341.8 1.0 copy.30
  (10 shorter events, 0.1 us)
Async XLA Ops:
  0.0 8.7 %copy-start = (f32[16,16384]{1,0:T(8,128)S(1)}, f32[16,16384]{1,0:T(8,128)}, u32[]{:S(2)}) copy-start(f32[16,16384]{1,0:T(8,128)} %param.6) | copy-start | bytes 3145732
  2.4 32.0 %all-to-all-start = ((f32[16,4,4096]{2,0,1:T(8,128)}), f32[16,4,4096]{2,0,1:T(8,128)S(1)}, u32[]{:S(2)}, u32[]{:S(2)}) async-start(f32[16,4,4096]{2,0,1:T(8,128)} %bitcast.59), calls=%async_computation | async-start | bytes 2097152 | tf_op jit(solution)/shard_map/all_to_all | solution.py:58
  34.4 28.7 %all-to-all-start.1 = ((f32[16,4,4096]{2,0,1:T(8,128)}), f32[16,4,4096]{2,0,1:T(8,128)S(1)}, u32[]{:S(2)}, u32[]{:S(2)}) async-start(f32[16,4,4096]{2,0,1:T(8,128)} %bitcast.58), calls=%async_computation.1 | async-start | bytes 2097152 | tf_op jit(solution)/shard_map/all_to_all | solution.py:53
  41.0 3.6 %copy-start.1 = (s32[2,2048]{1,0:T(2,128)S(1)}, s32[2,2048]{1,0:T(2,128)}, u32[]{:S(2)}) copy-start(s32[2,2048]{1,0:T(2,128)} %param.9) | copy-start | bytes 49156
  63.1 122.9 %all-to-all-start.2 = ((f32[16,4,4096]{2,0,1:T(8,128)}), f32[16,4,4096]{2,0,1:T(8,128)S(1)}, u32[]{:S(2)}, u32[]{:S(2)}) async-start(f32[16,4,4096]{2,0,1:T(8,128)} %copy.24), calls=%async_computation.2 | async-start | bytes 2097152 | tf_op jit(solution)/shard_map/all_to_all | solution.py:59
  66.8 5.8 %copy-start.3 = (s32[2,128]{1,0:T(2,128)S(1)}, s32[2,128]{1,0:T(2,128)}, u32[]{:S(2)}) copy-start(s32[2,128]{1,0:T(2,128)} %param.11) | copy-start | bytes 3076
  72.6 12.6 %copy-start.2 = (f32[2,2048]{1,0:T(2,128)S(1)}, f32[2,2048]{1,0:T(2,128)}, u32[]{:S(2)}) copy-start(f32[2,2048]{1,0:T(2,128)} %param.10) | copy-start | bytes 49156
  186.0 29.5 %all-to-all-start.5 = ((f32[16,4,4096]{2,0,1:T(8,128)}), f32[16,4,4096]{2,0,1:T(8,128)}, u32[]{:S(2)}, u32[]{:S(2)}) async-start(f32[16,4,4096]{2,0,1:T(8,128)} %copy.25), calls=%async_computation.5 | async-start | bytes 2097152 | tf_op jit(solution)/shard_map/all_to_all | solution.py:59
  243.9 28.3 %all-to-all-start.4 = ((f32[16,4,4096]{2,0,1:T(8,128)}), f32[16,4,4096]{2,0,1:T(8,128)S(1)}, u32[]{:S(2)}, u32[]{:S(2)}) async-start(f32[16,4,4096]{2,0,1:T(8,128)} %bitcast.72), calls=%async_computation.4 | async-start | bytes 2097152 | tf_op jit(solution)/shard_map/all_to_all | solution.py:58
where the time goes:
time: 344 us; the launch traced here: 343 us
  blocking collectives  136 us (40%)
  waiting for transfers between devices  89.9 us (26%)
  other arithmetic  48 us (14%)
  local copies, waits for them, and re-layouts  42.2 us (12%)
  starting transfers between devices  21.3 us (6%)
  matrix products  4.91 us (1%)
    psum x2, blocking collectives, advance(): cross, prior_sq = lax.psum((cross_part, prior_part), ('member', 'cell'))  78.9 us
    all_to_all x2, blocking collectives, per_device(): lax.all_to_all(slab, 'member', split_axis=0, concat_axis=1, tiled=True)  57.4 us
    all_to_all x2, waiting for transfers between devices, per_device(): lax.all_to_all(state, 'member', split_axis=1, concat_axis=0, tiled=True)  48.1 us
    gather x2, local copies, waits for them, and re-layouts, per_device(): weight = flags[where // 128]  25.2 us
    all_to_all x2, waiting for transfers between devices, per_device(): lax.all_to_all(noise[step], 'member', split_axis=1, concat_axis=0, tiled=...  23.2 us
    scatter-add x2, other arithmetic, per_device(): precision_field = precision_field.at[where].add(weight)  22.8 us
    scatter-add x2, other arithmetic, per_device(): target_field = target_field.at[where].add(weight * obs_values[survey])  22.8 us
    all_to_all x1, waiting for transfers between devices, per_device(): lax.all_to_all(prior, 'member', split_axis=1, concat_axis=0, tiled=True)  18.6 us
  transfers between devices with their start and end apart: 5, of which 4 were waited for; matrix products, arithmetic and copies ran while one was open for 25% of the time, Pallas kernels for 0%

commit v1 on v0

v1 whole, which is shorter than its diff:
```python
import functools
import math

import jax
import jax.numpy as jnp
from jax import lax
from jax.experimental import pallas as pl
from jax.experimental.pallas import tpu as pltpu
from jax.sharding import PartitionSpec as P

STEPS = 2
LANES = 128
CHUNKS = 8
OBS_CHUNK = 512
MESH = pl.DeviceIdType.MESH
NT = (((1,), (1,)), ((), ()))


def constants(step):
    time_now = 0.6 - 0.1 * step
    alpha = 1.0 - 0.95 * time_now
    drift = -0.95 / alpha
    diffusion = 1.0 - 2.0 * drift * time_now
    keep = 1.0 - 0.1 * drift - 0.1 * diffusion / time_now
    obs = 0.1 * diffusion * (1.0 - time_now)
    pull = 0.1 * diffusion * alpha / time_now
    spread = math.sqrt(0.1 * diffusion)
    return time_now, alpha, keep, obs, pull, spread


def split(x):
    high = x.astype(jnp.bfloat16)
    low = (x - high.astype(jnp.float32)).astype(jnp.bfloat16)
    return high, low


def softmax_rows(logits):
    top = jnp.max(logits, axis=1, keepdims=True)
    e = jnp.exp(logits - top)
    return e / jnp.sum(e, axis=1, keepdims=True)


def kernel(
    groups,
    shards,
    prior_ref,
    samples_ref,
    noise_ref,
    cells_ref,
    values_ref,
    mask_ref,
    out_ref,
    gath,
    samples_v,
    noise_v,
    split_sy,
    split_p,
    base_v,
    scale_v,
    result_v,
    field_v,
    acc,
    inbox,
    outbox,
    local_sem,
    out_sem,
    send_sem,
    recv_sem,
    red_send,
    red_recv,
):
    me = lax.axis_index("member")
    shard = lax.axis_index("cell")
    rows, cells = prior_ref.shape
    ens = rows * groups
    width = cells // CHUNKS
    ncell = cells * shards
    rounds = shards.bit_length() - 1

    def span(c):
        return pl.ds(pl.multiple_of(c * width, width), width)

    def hop(way, origin, c, own=False):
        target = me + 1 if way == 0 else me - 1
        block = gath.at[origin, :, span(c)]
        return pltpu.make_async_remote_copy(
            src_ref=prior_ref.at[:, span(c)] if own else block,
            dst_ref=block,
            send_sem=send_sem.at[way, origin, c],
            recv_sem=recv_sem.at[origin, c],
            device_id={"member": target},
            device_id_type=MESH,
        )

    def partner(r):
        bit = 1 << r
        return shard + bit * (1 - 2 * ((shard // bit) % 2))

    loads = [
        pltpu.make_async_copy(prior_ref, gath.at[me], local_sem.at[0]),
        pltpu.make_async_copy(samples_ref, samples_v, local_sem.at[1]),
        pltpu.make_async_copy(noise_ref, noise_v, local_sem.at[2]),
    ]
    for load in loads:
        load.start()

    barrier = pltpu.get_barrier_semaphore()

    @pl.when(me > 0)
    def _():
        pl.semaphore_signal(barrier, inc=1, device_id={"member": me - 1}, device_id_type=MESH)

    @pl.when(me < groups - 1)
    def _():
        pl.semaphore_signal(barrier, inc=1, device_id={"member": me + 1}, device_id_type=MESH)

    for r in range(rounds):
        pl.semaphore_signal(barrier, inc=1, device_id={"cell": partner(r)}, device_id_type=MESH)
    inner = (me > 0) & (me < groups - 1)

    @pl.when(inner)
    def _():
        pl.semaphore_wait(barrier, rounds + 2)

    @pl.when(jnp.logical_not(inner))
    def _():
        pl.semaphore_wait(barrier, rounds + 1)

    def send_own(c, _):
        @pl.when(me < groups - 1)
        def _():
            hop(0, me, c, own=True).start()

        @pl.when(me > 0)
        def _():
            hop(1, me, c, own=True).start()

        return 0

    lax.fori_loop(0, CHUNKS, send_own, 0)

    blocks = cells // LANES
    count_obs = cells_ref.shape[1]
    piece = min(OBS_CHUNK, count_obs)
    eye = lax.broadcasted_iota(jnp.int32, (blocks, blocks), 0) == lax.broadcasted_iota(
        jnp.int32, (blocks, blocks), 1
    )
    field_v[...] = jnp.zeros_like(field_v)
    for survey in range(cells_ref.shape[0]):

        def gather_obs(o, total, survey=survey):
            at = pl.ds(pl.multiple_of(o * piece, piece), piece)
            where = cells_ref[survey : survey + 1, at] - shard * cells
            values = values_ref[survey : survey + 1, at]
            block_of = where // LANES
            lane_of = where - block_of * LANES
            first = (
                lax.broadcasted_iota(jnp.int32, (blocks, piece), 0) == block_of
            )
            second = lax.broadcasted_iota(jnp.int32, (LANES, piece), 0) == lane_of
            one = values.astype(jnp.bfloat16).astype(jnp.float32)
            two = (values - one).astype(jnp.bfloat16).astype(jnp.float32)
            three = values - one - two
            left = jnp.where(first, 1.0, 0.0).astype(jnp.bfloat16)
            right = jnp.concatenate(
                [
                    jnp.where(second, part, 0.0).astype(jnp.bfloat16)
                    for part in (jnp.ones_like(values), one, two, three)
                ],
                axis=0,
            )
            return total + lax.dot_general(left, right, NT, preferred_element_type=jnp.float32)

        total = lax.fori_loop(
            0, count_obs // piece, gather_obs, jnp.zeros((blocks, 4 * LANES), jnp.float32)
        )
        flags = mask_ref[survey : survey + 1, :].astype(jnp.float32)
        column = jnp.sum(jnp.where(eye, flags, 0.0), axis=1, keepdims=True)
        field_v[0] += column * total[:, :LANES]
        field_v[1] += column * (
            total[:, LANES : 2 * LANES]
            + total[:, 2 * LANES : 3 * LANES]
            + total[:, 3 * LANES : 4 * LANES]
        )

    loads[1].wait()
    loads[2].wait()
    _, _, keep0, obs0, pull0, spread0 = constants(0)
    _, _, keep1, obs1, pull1, spread1 = constants(1)

    def prepare(h, _):
        at = pl.ds(pl.multiple_of(h * LANES, LANES), LANES)
        precision = field_v[0, pl.ds(h, 1), :]
        target = field_v[1, pl.ds(h, 1), :]
        state = samples_v[:, at]
        moved = (keep0 - obs0 * precision) * state + obs0 * target + spread0 * noise_v[0, :, at]
        factor = keep1 - obs1 * precision
        base_v[:, at] = factor * moved + obs1 * target + spread1 * noise_v[1, :, at]
        scale_v[:, at] = jnp.broadcast_to(pull0 * factor, (rows, LANES))
        high, low = split(jnp.concatenate([state, moved], axis=0))
        split_sy[: 2 * rows, at] = high
        split_sy[2 * rows :, at] = low
        return 0

    lax.fori_loop(0, blocks, prepare, 0)
    loads[0].wait()
    acc[...] = jnp.zeros_like(acc)

    def products(c):
        at = span(c)
        high, low = split(gath[:, :, at].reshape(ens, width))
        split_p[:ens, at] = high
        split_p[ens:, at] = low
        right = jnp.concatenate([high, low], axis=0)
        left = jnp.concatenate([split_sy[:, at], right], axis=0)
        acc[...] += lax.dot_general(left, right, NT, preferred_element_type=jnp.float32)

    for d in range(1, groups):

        def relay(c, _, d=d):
            @pl.when(me - d >= 0)
            def _():
                hop(1, me - d, c).wait_recv()

                @pl.when(me < groups - 1)
                def _():
                    hop(0, me - d, c).start()

            @pl.when(me + d < groups)
            def _():
                hop(0, me + d, c).wait_recv()

                @pl.when(me > 0)
                def _():
                    hop(1, me + d, c).start()

            if d == groups - 1:
                products(c)
            return 0

        lax.fori_loop(0, CHUNKS, relay, 0)

    whole = acc[...]
    four = 4 * rows
    sy = whole[: 2 * rows] + whole[2 * rows : four]
    gram = whole[four : four + ens] + whole[four + ens :]
    part = jnp.concatenate([sy, gram], axis=0)
    part = part[:, :ens] + part[:, ens:]
    half = part.shape[0] // 2
    part = jnp.concatenate([part[:half], part[half:]], axis=1)
    for r in range(rounds):
        outbox[r] = part
        swap = pltpu.make_async_remote_copy(
            src_ref=outbox.at[r],
            dst_ref=inbox.at[r],
            send_sem=red_send.at[r],
            recv_sem=red_recv.at[r],
            device_id={"cell": partner(r)},
            device_id_type=MESH,
        )
        swap.start()
        swap.wait()
        part = part + inbox[r]
    part = jnp.concatenate([part[:, :ens], part[:, ens:]], axis=0)
    cross0 = part[:rows]
    cross1 = part[rows : 2 * rows]
    gram = part[2 * rows :]
    diagonal = lax.broadcasted_iota(jnp.int32, (ens, ens), 0) == lax.broadcasted_iota(
        jnp.int32, (ens, ens), 1
    )
    prior_sq = jnp.sum(jnp.where(diagonal, gram, 0.0), axis=0, keepdims=True)

    def weigh(step, cross):
        time_now, alpha = constants(step)[:2]
        dist = alpha * alpha * prior_sq - 2.0 * alpha * cross
        return softmax_rows(-dist / (2.0 * time_now * math.sqrt(ncell)))

    weights0 = weigh(0, cross0)
    cross1 = cross1 + pull0 * jnp.dot(
        weights0, gram, precision=lax.Precision.HIGHEST, preferred_element_type=jnp.float32
    )
    weights1 = weigh(1, cross1)
    high, low = split(jnp.concatenate([weights0, weights1], axis=0))
    both = jnp.concatenate([high, low], axis=0)
    both = jnp.concatenate([both, both], axis=1)

    def store(c):
        return pltpu.make_async_copy(
            result_v.at[:, span(c)], out_ref.at[:, span(c)], out_sem.at[c]
        )

    def finish(c, _):
        at = span(c)
        mean = jnp.dot(both, split_p[:, at], preferred_element_type=jnp.float32)
        mean = mean[: 2 * rows] + mean[2 * rows :]
        result_v[:, at] = base_v[:, at] + scale_v[:, at] * mean[:rows] + pull1 * mean[rows:]
        store(c).start()
        return 0

    lax.fori_loop(0, CHUNKS, finish, 0)

    def drain(c, _):
        store(c).wait()
        for origin in range(groups):

            @pl.when((origin <= me) & (me < groups - 1))
            def _():
                hop(0, origin, c).wait_send()

            @pl.when((origin >= me) & (me > 0))
            def _():
                hop(1, origin, c).wait_send()

        return 0

    lax.fori_loop(0, CHUNKS, drain, 0)


def per_device(prior, samples, noise, obs_cells, obs_values, seismic_mask):
    rows, cells = prior.shape
    groups = lax.axis_size("member")
    shards = lax.axis_size("cell")
    ens = rows * groups
    rounds = shards.bit_length() - 1
    half = (2 * rows + ens) // 2
    hbm = pl.BlockSpec(memory_space=pl.ANY)
    vmem = pl.BlockSpec(memory_space=pltpu.VMEM)
    f32 = jnp.float32
    return pl.pallas_call(
        functools.partial(kernel, groups, shards),
        out_shape=jax.ShapeDtypeStruct((rows, cells), f32),
        in_specs=[hbm, hbm, hbm, vmem, vmem, vmem],
        out_specs=hbm,
        scratch_shapes=[
            pltpu.VMEM((groups, rows, cells), f32),
            pltpu.VMEM((rows, cells), f32),
            pltpu.VMEM((STEPS, rows, cells), f32),
            pltpu.VMEM((4 * rows, cells), jnp.bfloat16),
            pltpu.VMEM((2 * ens, cells), jnp.bfloat16),
            pltpu.VMEM((rows, cells), f32),
            pltpu.VMEM((rows, cells), f32),
            pltpu.VMEM((rows, cells), f32),
            pltpu.VMEM((2, cells // LANES, LANES), f32),
            pltpu.VMEM((4 * rows + 2 * ens, 2 * ens), f32),
            pltpu.VMEM((rounds, half, 2 * ens), f32),
            pltpu.VMEM((rounds, half, 2 * ens), f32),
            pltpu.SemaphoreType.DMA((3,)),
            pltpu.SemaphoreType.DMA((CHUNKS,)),
            pltpu.SemaphoreType.DMA((2, groups, CHUNKS)),
            pltpu.SemaphoreType.DMA((groups, CHUNKS)),
            pltpu.SemaphoreType.DMA((rounds,)),
            pltpu.SemaphoreType.DMA((rounds,)),
        ],
        compiler_params=pltpu.CompilerParams(
            collective_id=0, has_side_effects=True, vmem_limit_bytes=48 * 1024 * 1024
        ),
    )(prior, samples, noise, obs_cells, obs_values, seismic_mask)


def solution(mesh):
    in_specs = (
        P("member", "cell"),
        P("member", "cell"),
        P(None, "member", "cell"),
        P(None, "cell"),
        P(None, "cell"),
        P(None, "cell"),
    )
    out_specs = P("member", "cell")
    return jax.shard_map(
        per_device, mesh=mesh, in_specs=in_specs, out_specs=out_specs, check_vma=False
    )
```

time: 344 us -> 92.4 us (0.27)
  blocking collectives: 136 us -> 0 us
  waiting for transfers between devices: 89.9 us -> 0 us
  Pallas kernels: 0 us -> 84.9 us
  other arithmetic: 48 us -> 0 us
  local copies, waits for them, and re-layouts: 42.2 us -> 7.12 us
  starting transfers between devices: 21.3 us -> 0 us
  matrix products: 4.91 us -> 0 us
    all_to_all x5 -> x0, waiting for transfers between devices: 89.9 us -> none  [the longest x2 48.1 us: per_device(): lax.all_to_all(state, 'member', split_axis=1, concat_axis=0, tiled=True)]
    pallas_call x0 -> x1, Pallas kernels: none -> 84.9 us  [per_device(): pl.pallas_call(functools.partial(kernel, groups, shards), out_shape=jax.S...]
    psum x2 -> x0, blocking collectives: 78.9 us -> none  [advance(): cross, prior_sq = lax.psum((cross_part, prior_part), ('member', 'cell'))]
    all_to_all x2 -> x0, blocking collectives: 57.4 us -> none  [per_device(): lax.all_to_all(slab, 'member', split_axis=0, concat_axis=1, tiled=True)]
    scatter-add x4 -> x0, other arithmetic: 45.7 us -> none  [the longest x2 22.8 us: per_device(): precision_field = precision_field.at[where].add(weight)]
    gather x2 -> x0, local copies, waits for them, and re-layouts: 25.2 us -> none  [per_device(): weight = flags[where // 128]]
    all_to_all x5 -> x0, starting transfers between devices: 21.3 us -> none  [the longest x2 9.83 us: per_device(): lax.all_to_all(state, 'member', split_axis=1, concat_axis=0, tiled=True)]
    all_to_all x7 -> x0, local copies, waits for them, and re-layouts: 13.8 us -> none  [the longest x4 9.32 us: per_device(): lax.all_to_all(noise[step], 'member', split_axis=1, concat_axis=0, tiled=...]
  transfers between devices with their start and end apart: 5 -> 0, of which waited for: 4 -> 0; matrix products, arithmetic and copies ran while one was open for 25% -> 0% of each run, Pallas kernels for 0% -> 0%
where the time goes in v1:
time: 92.4 us; the launch traced here: 92 us
  Pallas kernels  84.9 us (92%)
  local copies, waits for them, and re-layouts  7.12 us (8%)
    pallas_call x1, Pallas kernels, per_device(): pl.pallas_call(functools.partial(kernel, groups, shards), out_shape=jax.S...  84.9 us
    unnamed x13, local copies, waits for them, and re-layouts  7.12 us

profile of v1, /device:TPU:0, one launch (start us, length us, event | category | flops | bytes accessed | tf_op | source)
XLA Modules:
  0.0 92.0 jit_solution(1917567400066652708)
XLA Ops:
  0.0 0.0 copy-start
  0.0 1.6 %copy-done = f32[2,16,16384]{2,1,0:T(8,128)S(1)} copy-done((f32[2,16,16384]{2,1,0:T(8,128)S(1)}, f32[2,16,16384]{2,1,0:T(8,128)}, u32[]{:S(2)}) %copy-start) | copy-done | bytes 2097176
  1.6 0.0 copy-start.1
  1.6 1.2 %copy-done.1 = f32[16,16384]{1,0:T(8,128)S(1)} copy-done((f32[16,16384]{1,0:T(8,128)S(1)}, f32[16,16384]{1,0:T(8,128)}, u32[]{:S(2)}) %copy-start.1) | copy-done | bytes 1048600
  2.8 0.0 copy-start.2
  2.8 1.2 %copy-done.2 = f32[16,16384]{1,0:T(8,128)S(1)} copy-done((f32[16,16384]{1,0:T(8,128)S(1)}, f32[16,16384]{1,0:T(8,128)}, u32[]{:S(2)}) %copy-start.2) | copy-done | bytes 1048600
  4.0 0.0 copy-start.3
  4.0 0.7 copy-done.3
  4.8 0.0 copy-start.4
  4.8 0.7 copy-done.4
  5.5 0.0 copy-start.5
  5.5 0.7 copy-done.5
  6.2 84.9 %shard_map.64 = f32[16,16384]{1,0:T(8,128)S(1)} custom-call(f32[16,16384]{1,0:T(8,128)S(1)} %copy-done.1, f32[16,16384]{1,0:T(8,128)S(1)} %copy-done.2, f32[2,16,16384]{2,1,0:T(8,128)S(1)} %copy-done, s32[2,2048]{1,0:T(2,128)S(1)} %copy-done.3, f32[2,2048]{1,0:T(2,128)S(1)} %copy-done.4, s32[2,128]{1,0:T(2,128)S(1)} %copy-done.5), custom_call_target="tpu_custom_call" | custom-call | tf_op jit(solution)/shard_map/pallas_call | solution.py:329
  91.1 1.0 %copy.8 = f32[16,16384]{1,0:T(8,128)} copy(f32[16,16384]{1,0:T(8,128)S(1)} %shard_map.64) | data formatting | bytes 2097152
Async XLA Ops:
  0.0 1.6 %copy-start = (f32[2,16,16384]{2,1,0:T(8,128)S(1)}, f32[2,16,16384]{2,1,0:T(8,128)}, u32[]{:S(2)}) copy-start(f32[2,16,16384]{2,1,0:T(8,128)} %noise_ref.1) | copy-start | bytes 6291460
  1.6 1.2 %copy-start.1 = (f32[16,16384]{1,0:T(8,128)S(1)}, f32[16,16384]{1,0:T(8,128)}, u32[]{:S(2)}) copy-start(f32[16,16384]{1,0:T(8,128)} %prior_ref.1) | copy-start | bytes 3145732
  2.8 1.2 %copy-start.2 = (f32[16,16384]{1,0:T(8,128)S(1)}, f32[16,16384]{1,0:T(8,128)}, u32[]{:S(2)}) copy-start(f32[16,16384]{1,0:T(8,128)} %samples_ref.1) | copy-start | bytes 3145732
  4.0 0.7 copy-start.3
  4.8 0.7 copy-start.4
  5.5 0.7 copy-start.5

commit v2 on v1

--- a/solution.py
+++ b/solution.py
@@ -10,7 +10,8 @@
 
 STEPS = 2
 LANES = 128
-CHUNKS = 8
+CHUNKS = 16
+GUEST = 5
 OBS_CHUNK = 512
 MESH = pl.DeviceIdType.MESH
 NT = (((1,), (1,)), ((), ()))
@@ -50,6 +51,9 @@
     values_ref,
     mask_ref,
     out_ref,
+    cells_v,
+    values_v,
+    mask_v,
     gath,
     samples_v,
     noise_v,
@@ -68,6 +72,17 @@
     recv_sem,
     red_send,
     red_recv,
+    guest_in,
+    guest_sy,
+    guest_out,
+    guest_mean,
+    guest_acc,
+    guest_part,
+    guest_weights,
+    guest_send,
+    guest_recv,
+    mean_send,
+    mean_recv,
 ):
     me = lax.axis_index("member")
     shard = lax.axis_index("cell")
@@ -76,6 +91,11 @@
     width = cells // CHUNKS
     ncell = cells * shards
     rounds = shards.bit_length() - 1
+    low = 1 - (2 * me) // groups
+    end = (me == 0) | (me == groups - 1)
+    helper = (me == 1) | (me == groups - 2)
+    outward = 1 - 2 * low
+    held = GUEST * width
 
     def span(c):
         return pl.ds(pl.multiple_of(c * width, width), width)
@@ -92,6 +112,47 @@
             device_id_type=MESH,
         )
 
+    def to_helper(i):
+        source = samples_ref if i == 0 else noise_ref.at[0]
+        return pltpu.make_async_remote_copy(
+            src_ref=source.at[:, :held],
+            dst_ref=guest_in.at[i],
+            send_sem=guest_send.at[i],
+            recv_sem=guest_recv.at[i],
+            device_id={"member": me - outward},
+            device_id_type=MESH,
+        )
+
+    def part_to_end(way=1):
+        return pltpu.make_async_remote_copy(
+            src_ref=guest_part.at[0],
+            dst_ref=guest_part.at[1],
+            send_sem=guest_send.at[2],
+            recv_sem=guest_recv.at[2],
+            device_id={"member": me + way * outward},
+            device_id_type=MESH,
+        )
+
+    def weights_to_helper():
+        return pltpu.make_async_remote_copy(
+            src_ref=guest_weights.at[0],
+            dst_ref=guest_weights.at[1],
+            send_sem=guest_send.at[3],
+            recv_sem=guest_recv.at[3],
+            device_id={"member": me - outward},
+            device_id_type=MESH,
+        )
+
+    def mean_to_end(c, way=1):
+        return pltpu.make_async_remote_copy(
+            src_ref=guest_out.at[:, span(c)],
+            dst_ref=guest_mean.at[:, span(c)],
+            send_sem=mean_send.at[c],
+            recv_sem=mean_recv.at[c],
+            device_id={"member": me + way * outward},
+            device_id_type=MESH,
+        )
+
     def partner(r):
         bit = 1 << r
         return shard + bit * (1 - 2 * ((shard // bit) % 2))
@@ -100,6 +161,9 @@
         pltpu.make_async_copy(prior_ref, gath.at[me], local_sem.at[0]),
         pltpu.make_async_copy(samples_ref, samples_v, local_sem.at[1]),
         pltpu.make_async_copy(noise_ref, noise_v, local_sem.at[2]),
+        pltpu.make_async_copy(cells_ref, cells_v, local_sem.at[3]),
+        pltpu.make_async_copy(values_ref, values_v, local_sem.at[4]),
+        pltpu.make_async_copy(mask_ref, mask_v, local_sem.at[5]),
     ]
     for load in loads:
         load.start()
@@ -126,18 +190,28 @@
     def _():
         pl.semaphore_wait(barrier, rounds + 1)
 
-    def send_own(c, _):
-        @pl.when(me < groups - 1)
-        def _():
-            hop(0, me, c, own=True).start()
-
-        @pl.when(me > 0)
-        def _():
-            hop(1, me, c, own=True).start()
-
-        return 0
-
-    lax.fori_loop(0, CHUNKS, send_own, 0)
+    @pl.when(end)
+    def _():
+        to_helper(0).start()
+        to_helper(1).start()
+
+    def goes(way, c_held):
+        rim = 1 if c_held else 0
+        return me < groups - 1 - rim if way == 0 else me > rim
+
+    def send_own(c, _, c_held):
+        for way in range(2):
+
+            @pl.when(goes(way, c_held))
+            def _(way=way):
+                hop(way, me, c, own=True).start()
+
+        return 0
+
+    lax.fori_loop(0, GUEST, functools.partial(send_own, c_held=True), 0)
+    lax.fori_loop(GUEST, CHUNKS, functools.partial(send_own, c_held=False), 0)
+    for load in loads[3:]:
+        load.wait()
 
     blocks = cells // LANES
     count_obs = cells_ref.shape[1]
@@ -150,8 +224,8 @@
 
         def gather_obs(o, total, survey=survey):
             at = pl.ds(pl.multiple_of(o * piece, piece), piece)
-            where = cells_ref[survey : survey + 1, at] - shard * cells
-            values = values_ref[survey : survey + 1, at]
+            where = cells_v[survey : survey + 1, at] - shard * cells
+            values = values_v[survey : survey + 1, at]
             block_of = where // LANES
             lane_of = where - block_of * LANES
             first = (
@@ -174,7 +248,7 @@
         total = lax.fori_loop(
             0, count_obs // piece, gather_obs, jnp.zeros((blocks, 4 * LANES), jnp.float32)
         )
-        flags = mask_ref[survey : survey + 1, :].astype(jnp.float32)
+        flags = mask_v[survey : survey + 1, :].astype(jnp.float32)
         column = jnp.sum(jnp.where(eye, flags, 0.0), axis=1, keepdims=True)
         field_v[0] += column * total[:, :LANES]
         field_v[1] += column * (
@@ -188,12 +262,15 @@
     _, _, keep0, obs0, pull0, spread0 = constants(0)
     _, _, keep1, obs1, pull1, spread1 = constants(1)
 
+    def advance(state, fresh, precision, target):
+        return (keep0 - obs0 * precision) * state + obs0 * target + spread0 * fresh
+
     def prepare(h, _):
         at = pl.ds(pl.multiple_of(h * LANES, LANES), LANES)
         precision = field_v[0, pl.ds(h, 1), :]
         target = field_v[1, pl.ds(h, 1), :]
         state = samples_v[:, at]
-        moved = (keep0 - obs0 * precision) * state + obs0 * target + spread0 * noise_v[0, :, at]
+        moved = advance(state, noise_v[0, :, at], precision, target)
         factor = keep1 - obs1 * precision
         base_v[:, at] = factor * moved + obs1 * target + spread1 * noise_v[1, :, at]
         scale_v[:, at] = jnp.broadcast_to(pull0 * factor, (rows, LANES))
@@ -202,54 +279,102 @@
         split_sy[2 * rows :, at] = low
         return 0
 
+    def prepare_guest(h, _):
+        at = pl.ds(pl.multiple_of(h * LANES, LANES), LANES)
+        precision = field_v[0, pl.ds(h, 1), :]
+        target = field_v[1, pl.ds(h, 1), :]
+        state = guest_in[0, :, at]
+        moved = advance(state, guest_in[1, :, at], precision, target)
+        high, low = split(jnp.concatenate([state, moved], axis=0))
+        guest_sy[: 2 * rows, at] = high
+        guest_sy[2 * rows :, at] = low
+        return 0
+
     lax.fori_loop(0, blocks, prepare, 0)
     loads[0].wait()
     acc[...] = jnp.zeros_like(acc)
 
-    def products(c):
+    four = 4 * rows
+
+    def products(c, guest):
         at = span(c)
         high, low = split(gath[:, :, at].reshape(ens, width))
         split_p[:ens, at] = high
         split_p[ens:, at] = low
         right = jnp.concatenate([high, low], axis=0)
-        left = jnp.concatenate([split_sy[:, at], right], axis=0)
-        acc[...] += lax.dot_general(left, right, NT, preferred_element_type=jnp.float32)
+        first = [split_sy[:, at], guest_sy[:, at]] if guest else [split_sy[:, at]]
+        left = jnp.concatenate(first + [right], axis=0)
+        total = guest_acc if guest else acc
+        total[...] += lax.dot_general(left, right, NT, preferred_element_type=jnp.float32)
+
+    def fold(sy, gram):
+        part = jnp.concatenate(
+            [sy[: 2 * rows] + sy[2 * rows :], gram[:ens] + gram[ens:]], axis=0
+        )
+        part = part[:, :ens] + part[:, ens:]
+        half = part.shape[0] // 2
+        return jnp.concatenate([part[:half], part[half:]], axis=1)
+
+    def relay(c, _, d, c_held):
+        comes = (me < groups - 1, me > 0) if c_held else (True, True)
+
+        @pl.when((me - d >= 0) & comes[0])
+        def _():
+            hop(1, me - d, c).wait_recv()
+
+            @pl.when(goes(0, c_held))
+            def _():
+                hop(0, me - d, c).start()
+
+        @pl.when((me + d < groups) & comes[1])
+        def _():
+            hop(0, me + d, c).wait_recv()
+
+            @pl.when(goes(1, c_held))
+            def _():
+                hop(1, me + d, c).start()
+
+        if 2 * d >= groups and not (c_held and d == groups - 1):
+
+            @pl.when((me == d) | (me == groups - 1 - d))
+            def _():
+                products(c, c_held and d == groups - 2)
+
+        return 0
 
     for d in range(1, groups):
-
-        def relay(c, _, d=d):
-            @pl.when(me - d >= 0)
+        if d == groups - 2:
+
+            @pl.when(helper)
             def _():
-                hop(1, me - d, c).wait_recv()
-
-                @pl.when(me < groups - 1)
-                def _():
-                    hop(0, me - d, c).start()
-
-            @pl.when(me + d < groups)
+                to_helper(0).wait_recv()
+                to_helper(1).wait_recv()
+                guest_acc[...] = jnp.zeros_like(guest_acc)
+                lax.fori_loop(0, held // LANES, prepare_guest, 0)
+
+        lax.fori_loop(0, GUEST, functools.partial(relay, d=d, c_held=True), 0)
+        if d == groups - 2:
+
+            @pl.when(helper)
             def _():
-                hop(0, me + d, c).wait_recv()
-
-                @pl.when(me > 0)
-                def _():
-                    hop(1, me + d, c).start()
-
-            if d == groups - 1:
-                products(c)
-            return 0
-
-        lax.fori_loop(0, CHUNKS, relay, 0)
-
-    whole = acc[...]
-    four = 4 * rows
-    sy = whole[: 2 * rows] + whole[2 * rows : four]
-    gram = whole[four : four + ens] + whole[four + ens :]
-    part = jnp.concatenate([sy, gram], axis=0)
-    part = part[:, :ens] + part[:, ens:]
-    half = part.shape[0] // 2
-    part = jnp.concatenate([part[:half], part[half:]], axis=1)
+                acc[:four] = guest_acc[:four]
+                acc[four:] = guest_acc[2 * four :]
+                guest_part[0] = fold(guest_acc[four : 2 * four], guest_acc[2 * four :])
+                part_to_end().start()
+
+        lax.fori_loop(GUEST, CHUNKS, functools.partial(relay, d=d, c_held=False), 0)
+
+    outbox[0] = fold(acc[:four], acc[four:])
+
+    @pl.when(end)
+    def _():
+        part_to_end(-1).wait_recv()
+        outbox[0] += guest_part[1]
+
+    part = outbox[0]
     for r in range(rounds):
-        outbox[r] = part
+        if r > 0:
+            outbox[r] = part
         swap = pltpu.make_async_remote_copy(
             src_ref=outbox.at[r],
             dst_ref=inbox.at[r],
@@ -280,9 +405,36 @@
         weights0, gram, precision=lax.Precision.HIGHEST, preferred_element_type=jnp.float32
     )
     weights1 = weigh(1, cross1)
-    high, low = split(jnp.concatenate([weights0, weights1], axis=0))
-    both = jnp.concatenate([high, low], axis=0)
-    both = jnp.concatenate([both, both], axis=1)
+    weights = jnp.concatenate([weights0, weights1], axis=0)
+
+    @pl.when(end)
+    def _():
+        guest_weights[0] = jnp.concatenate([weights, weights], axis=1)
+        weights_to_helper().start()
+
+    def stack(high, low):
+        both = jnp.concatenate([high, low], axis=0)
+        return both if both.shape[1] == 2 * ens else jnp.concatenate([both, both], axis=1)
+
+    def means(both, c):
+        at = span(c)
+        mean = jnp.dot(both, split_p[:, at], preferred_element_type=jnp.float32)
+        mean = mean[: 2 * rows] + mean[2 * rows :]
+        return scale_v[:, at] * mean[:rows] + pull1 * mean[rows:]
+
+    @pl.when(helper)
+    def _():
+        weights_to_helper().wait_recv()
+        guest_both = stack(*split(guest_weights[1]))
+
+        def serve(c, _):
+            guest_out[:, span(c)] = means(guest_both, c)
+            mean_to_end(c).start()
+            return 0
+
+        lax.fori_loop(0, GUEST, serve, 0)
+
+    both = stack(*split(weights))
 
     def store(c):
         return pltpu.make_async_copy(
@@ -291,29 +443,56 @@
 
     def finish(c, _):
         at = span(c)
-        mean = jnp.dot(both, split_p[:, at], preferred_element_type=jnp.float32)
-        mean = mean[: 2 * rows] + mean[2 * rows :]
-        result_v[:, at] = base_v[:, at] + scale_v[:, at] * mean[:rows] + pull1 * mean[rows:]
+        result_v[:, at] = base_v[:, at] + means(both, c)
         store(c).start()
         return 0
 
-    lax.fori_loop(0, CHUNKS, finish, 0)
-
-    def drain(c, _):
+    def finish_held(c, _):
+        at = span(c)
+        mean_to_end(c, -1).wait_recv()
+        result_v[:, at] = base_v[:, at] + guest_mean[:, at]
+        store(c).start()
+        return 0
+
+    lax.fori_loop(GUEST, CHUNKS, finish, 0)
+
+    @pl.when(end)
+    def _():
+        lax.fori_loop(0, GUEST, finish_held, 0)
+        to_helper(0).wait_send()
+        to_helper(1).wait_send()
+        weights_to_helper().wait_send()
+
+    @pl.when(jnp.logical_not(end))
+    def _():
+        lax.fori_loop(0, GUEST, finish, 0)
+
+    @pl.when(helper)
+    def _():
+        part_to_end().wait_send()
+
+    def drain(c, _, c_held):
         store(c).wait()
         for origin in range(groups):
 
-            @pl.when((origin <= me) & (me < groups - 1))
+            @pl.when((origin <= me) & goes(0, c_held))
+            def _(origin=origin):
+                hop(0, origin, c).wait_send()
+
+            @pl.when((origin >= me) & goes(1, c_held))
+            def _(origin=origin):
+                hop(1, origin, c).wait_send()
+
+        if c_held:
+
+            @pl.when(helper)
             def _():
-                hop(0, origin, c).wait_send()
-
-            @pl.when((origin >= me) & (me > 0))
-            def _():
-                hop(1, origin, c).wait_send()
-
-        return 0
-
-    lax.fori_loop(0, CHUNKS, drain, 0)
+                mean_to_end(c).wait_send()
+
+        return 0
+
+    lax.fori_loop(0, GUEST, functools.partial(drain, c_held=True), 0)
+    lax.fori_loop(GUEST, CHUNKS, functools.partial(drain, c_held=False), 0)
 
 
 def per_device(prior, samples, noise, obs_cells, obs_values, seismic_mask):
@@ -323,15 +502,18 @@
     ens = rows * groups
     rounds = shards.bit_length() - 1
     half = (2 * rows + ens) // 2
+    held = GUEST * (cells // CHUNKS)
     hbm = pl.BlockSpec(memory_space=pl.ANY)
-    vmem = pl.BlockSpec(memory_space=pltpu.VMEM)
     f32 = jnp.float32
     return pl.pallas_call(
         functools.partial(kernel, groups, shards),
         out_shape=jax.ShapeDtypeStruct((rows, cells), f32),
-        in_specs=[hbm, hbm, hbm, vmem, vmem, vmem],
+        in_specs=[hbm] * 6,
         out_specs=hbm,
         scratch_shapes=[
+            pltpu.VMEM(obs_cells.shape, jnp.int32),
+            pltpu.VMEM(obs_values.shape, f32),
+            pltpu.VMEM(seismic_mask.shape, jnp.int32),
             pltpu.VMEM((groups, rows, cells), f32),
             pltpu.VMEM((rows, cells), f32),
             pltpu.VMEM((STEPS, rows, cells), f32),
@@ -344,15 +526,26 @@
             pltpu.VMEM((4 * rows + 2 * ens, 2 * ens), f32),
             pltpu.VMEM((rounds, half, 2 * ens), f32),
             pltpu.VMEM((rounds, half, 2 * ens), f32),
-            pltpu.SemaphoreType.DMA((3,)),
+            pltpu.SemaphoreType.DMA((6,)),
             pltpu.SemaphoreType.DMA((CHUNKS,)),
             pltpu.SemaphoreType.DMA((2, groups, CHUNKS)),
             pltpu.SemaphoreType.DMA((groups, CHUNKS)),
             pltpu.SemaphoreType.DMA((rounds,)),
             pltpu.SemaphoreType.DMA((rounds,)),
+            pltpu.VMEM((2, rows, held), f32),
+            pltpu.VMEM((4 * rows, held), jnp.bfloat16),
+            pltpu.VMEM((rows, held), f32),
+            pltpu.VMEM((rows, held), f32),
+            pltpu.VMEM((8 * rows + 2 * ens, 2 * ens), f32),
+            pltpu.VMEM((2, half, 2 * ens), f32),
+            pltpu.VMEM((2, 2 * rows, 2 * ens), f32),
+            pltpu.SemaphoreType.DMA((4,)),
+            pltpu.SemaphoreType.DMA((4,)),
+            pltpu.SemaphoreType.DMA((GUEST,)),
+            pltpu.SemaphoreType.DMA((GUEST,)),
         ],
         compiler_params=pltpu.CompilerParams(
-            collective_id=0, has_side_effects=True, vmem_limit_bytes=48 * 1024 * 1024
+            collective_id=0, has_side_effects=True, vmem_limit_bytes=60 * 1024 * 1024
         ),
     )(prior, samples, noise, obs_cells, obs_values, seismic_mask)
 

time: 92.4 us -> 84.1 us (0.910)
  local copies, waits for them, and re-layouts: 7.12 us -> 2.26 us
  Pallas kernels: 84.9 us -> 81.7 us
    unnamed x13 -> x1, local copies, waits for them, and re-layouts: 7.12 us -> 2.26 us
    pallas_call x1, Pallas kernels: 84.9 us -> 81.7 us  [per_device(): pl.pallas_call(functools.partial(kernel, groups, shards), out_shape=jax.S...]
where the time goes in v2:
time: 84.1 us; the launch traced here: 84 us
  Pallas kernels  81.7 us (97%)
  local copies, waits for them, and re-layouts  2.26 us (3%)
    pallas_call x1, Pallas kernels, per_device(): pl.pallas_call(functools.partial(kernel, groups, shards), out_shape=jax.S...  81.7 us
    unnamed x1, local copies, waits for them, and re-layouts  2.26 us

profile of v2, /device:TPU:0, one launch (start us, length us, event | category | flops | bytes accessed | tf_op | source)
XLA Modules:
  0.0 84.0 jit_solution(13725693144662834536)
XLA Ops:
  0.0 81.7 %shard_map.64 = f32[16,16384]{1,0:T(8,128)} custom-call(f32[16,16384]{1,0:T(8,128)} %prior_ref.1, f32[16,16384]{1,0:T(8,128)} %samples_ref.1, f32[2,16,16384]{2,1,0:T(8,128)} %noise_ref.1, s32[2,2048]{1,0:T(2,128)} %cells_ref.1, f32[2,2048]{1,0:T(2,128)} %values_ref.1, s32[2,128]{1,0:T(2,128)} %mask_ref.1), custom_call_target="tpu_custom_call" | custom-call | tf_op jit(solution)/shard_map/pallas_call | solution.py:508
  81.7 2.3 %copy.8 = f32[16,16384]{1,0:T(8,128)} copy(f32[16,16384]{1,0:T(8,128)} %shard_map.64) | data formatting | bytes 2097152

commit v3 on v2

--- a/solution.py
+++ b/solution.py
@@ -11,7 +11,10 @@
 STEPS = 2
 LANES = 128
 CHUNKS = 16
-GUEST = 5
+THIRD = 3
+GUEST = CHUNKS // THIRD
+LAG = 2
+AHEAD = 8
 OBS_CHUNK = 512
 MESH = pl.DeviceIdType.MESH
 NT = (((1,), (1,)), ((), ()))
@@ -79,6 +82,8 @@
     guest_acc,
     guest_part,
     guest_weights,
+    in_send,
+    in_recv,
     guest_send,
     guest_recv,
     mean_send,
@@ -95,7 +100,8 @@
     end = (me == 0) | (me == groups - 1)
     helper = (me == 1) | (me == groups - 2)
     outward = 1 - 2 * low
-    held = GUEST * width
+    furthest = me + low * (groups - 1 - 2 * me)
+    steps = CHUNKS + LAG * (groups - 1)
 
     def span(c):
         return pl.ds(pl.multiple_of(c * width, width), width)
@@ -112,13 +118,16 @@
             device_id_type=MESH,
         )
 
-    def to_helper(i):
+    def left_out(c):
+        return c % THIRD == 1
+
+    def to_helper(i, g):
         source = samples_ref if i == 0 else noise_ref.at[0]
         return pltpu.make_async_remote_copy(
-            src_ref=source.at[:, :held],
-            dst_ref=guest_in.at[i],
-            send_sem=guest_send.at[i],
-            recv_sem=guest_recv.at[i],
+            src_ref=source.at[:, span(THIRD * g + 1)],
+            dst_ref=guest_in.at[i, :, span(g)],
+            send_sem=in_send.at[i, g],
+            recv_sem=in_recv.at[i, g],
             device_id={"member": me - outward},
             device_id_type=MESH,
         )
@@ -127,8 +136,8 @@
         return pltpu.make_async_remote_copy(
             src_ref=guest_part.at[0],
             dst_ref=guest_part.at[1],
-            send_sem=guest_send.at[2],
-            recv_sem=guest_recv.at[2],
+            send_sem=guest_send.at[0],
+            recv_sem=guest_recv.at[0],
             device_id={"member": me + way * outward},
             device_id_type=MESH,
         )
@@ -137,18 +146,18 @@
         return pltpu.make_async_remote_copy(
             src_ref=guest_weights.at[0],
             dst_ref=guest_weights.at[1],
-            send_sem=guest_send.at[3],
-            recv_sem=guest_recv.at[3],
+            send_sem=guest_send.at[1],
+            recv_sem=guest_recv.at[1],
             device_id={"member": me - outward},
             device_id_type=MESH,
         )
 
-    def mean_to_end(c, way=1):
+    def mean_to_end(g, way=1):
         return pltpu.make_async_remote_copy(
-            src_ref=guest_out.at[:, span(c)],
-            dst_ref=guest_mean.at[:, span(c)],
-            send_sem=mean_send.at[c],
-            recv_sem=mean_recv.at[c],
+            src_ref=guest_out.at[:, span(g)],
+            dst_ref=guest_mean.at[:, span(g)],
+            send_sem=mean_send.at[g],
+            recv_sem=mean_recv.at[g],
             device_id={"member": me + way * outward},
             device_id_type=MESH,
         )
@@ -190,26 +199,33 @@
     def _():
         pl.semaphore_wait(barrier, rounds + 1)
 
-    @pl.when(end)
-    def _():
-        to_helper(0).start()
-        to_helper(1).start()
-
-    def goes(way, c_held):
-        rim = 1 if c_held else 0
-        return me < groups - 1 - rim if way == 0 else me > rim
-
-    def send_own(c, _, c_held):
+    def goes(way, c):
+        if way == 0:
+            return (me < groups - 2) | ((me < groups - 1) & jnp.logical_not(left_out(c)))
+        return (me > 1) | ((me > 0) & jnp.logical_not(left_out(c)))
+
+    def send_own(c):
         for way in range(2):
 
-            @pl.when(goes(way, c_held))
+            @pl.when(goes(way, c))
             def _(way=way):
                 hop(way, me, c, own=True).start()
 
+    def begin(c, _):
+        send_own(c)
         return 0
 
-    lax.fori_loop(0, GUEST, functools.partial(send_own, c_held=True), 0)
-    lax.fori_loop(GUEST, CHUNKS, functools.partial(send_own, c_held=False), 0)
+    lax.fori_loop(0, AHEAD, begin, 0)
+
+    @pl.when(end)
+    def _():
+        def give(g, _):
+            to_helper(0, g).start()
+            to_helper(1, g).start()
+            return 0
+
+        lax.fori_loop(0, GUEST, give, 0)
+
     for load in loads[3:]:
         load.wait()
 
@@ -279,20 +295,29 @@
         split_sy[2 * rows :, at] = low
         return 0
 
-    def prepare_guest(h, _):
-        at = pl.ds(pl.multiple_of(h * LANES, LANES), LANES)
-        precision = field_v[0, pl.ds(h, 1), :]
-        target = field_v[1, pl.ds(h, 1), :]
-        state = guest_in[0, :, at]
-        moved = advance(state, guest_in[1, :, at], precision, target)
-        high, low = split(jnp.concatenate([state, moved], axis=0))
-        guest_sy[: 2 * rows, at] = high
-        guest_sy[2 * rows :, at] = low
-        return 0
+    def prepare_guest(c):
+        g = c // THIRD
+        to_helper(0, g).wait_recv()
+        to_helper(1, g).wait_recv()
+
+        def one(k, _):
+            h = c * (width // LANES) + k
+            at = pl.ds(pl.multiple_of(g * width + k * LANES, LANES), LANES)
+            precision = field_v[0, pl.ds(h, 1), :]
+            target = field_v[1, pl.ds(h, 1), :]
+            state = guest_in[0, :, at]
+            moved = advance(state, guest_in[1, :, at], precision, target)
+            high, low = split(jnp.concatenate([state, moved], axis=0))
+            guest_sy[: 2 * rows, at] = high
+            guest_sy[2 * rows :, at] = low
+            return 0
+
+        lax.fori_loop(0, width // LANES, one, 0)
 
     lax.fori_loop(0, blocks, prepare, 0)
     loads[0].wait()
     acc[...] = jnp.zeros_like(acc)
+    guest_acc[...] = jnp.zeros_like(guest_acc)
 
     four = 4 * rows
 
@@ -302,7 +327,7 @@
         split_p[:ens, at] = high
         split_p[ens:, at] = low
         right = jnp.concatenate([high, low], axis=0)
-        first = [split_sy[:, at], guest_sy[:, at]] if guest else [split_sy[:, at]]
+        first = [split_sy[:, at], guest_sy[:, span(c // THIRD)]] if guest else [split_sy[:, at]]
         left = jnp.concatenate(first + [right], axis=0)
         total = guest_acc if guest else acc
         total[...] += lax.dot_general(left, right, NT, preferred_element_type=jnp.float32)
@@ -315,54 +340,65 @@
         half = part.shape[0] // 2
         return jnp.concatenate([part[:half], part[half:]], axis=1)
 
-    def relay(c, _, d, c_held):
-        comes = (me < groups - 1, me > 0) if c_held else (True, True)
-
-        @pl.when((me - d >= 0) & comes[0])
+    def relay(c, d):
+        missing = left_out(c)
+
+        @pl.when((me - d >= 0) & ((me < groups - 1) | jnp.logical_not(missing)))
         def _():
             hop(1, me - d, c).wait_recv()
 
-            @pl.when(goes(0, c_held))
+            @pl.when(goes(0, c))
             def _():
                 hop(0, me - d, c).start()
 
-        @pl.when((me + d < groups) & comes[1])
+        @pl.when((me + d < groups) & ((me > 0) | jnp.logical_not(missing)))
         def _():
             hop(0, me + d, c).wait_recv()
 
-            @pl.when(goes(1, c_held))
+            @pl.when(goes(1, c))
             def _():
                 hop(1, me + d, c).start()
 
-        if 2 * d >= groups and not (c_held and d == groups - 1):
-
-            @pl.when((me == d) | (me == groups - 1 - d))
+    def step(t, _):
+        @pl.when(t + AHEAD < CHUNKS)
+        def _():
+            send_own(t + AHEAD)
+
+        for d in range(1, groups):
+            c = t - LAG * d
+
+            @pl.when((c >= 0) & (c < CHUNKS))
+            def _(c=c, d=d):
+                relay(c, d)
+
+        c = t - LAG * furthest
+
+        @pl.when((c >= 0) & (c < CHUNKS))
+        def _():
+            missing = left_out(c)
+
+            @pl.when(missing & helper)
             def _():
-                products(c, c_held and d == groups - 2)
+                prepare_guest(c)
+                products(c, True)
+
+                @pl.when(c == THIRD * GUEST - 2)
+                def _():
+                    guest_part[0] = fold(guest_acc[four : 2 * four], guest_acc[2 * four :])
+                    part_to_end().start()
+
+            @pl.when(jnp.logical_not(missing & (end | helper)))
+            def _():
+                products(c, False)
 
         return 0
 
-    for d in range(1, groups):
-        if d == groups - 2:
-
-            @pl.when(helper)
-            def _():
-                to_helper(0).wait_recv()
-                to_helper(1).wait_recv()
-                guest_acc[...] = jnp.zeros_like(guest_acc)
-                lax.fori_loop(0, held // LANES, prepare_guest, 0)
-
-        lax.fori_loop(0, GUEST, functools.partial(relay, d=d, c_held=True), 0)
-        if d == groups - 2:
-
-            @pl.when(helper)
-            def _():
-                acc[:four] = guest_acc[:four]
-                acc[four:] = guest_acc[2 * four :]
-                guest_part[0] = fold(guest_acc[four : 2 * four], guest_acc[2 * four :])
-                part_to_end().start()
-
-        lax.fori_loop(GUEST, CHUNKS, functools.partial(relay, d=d, c_held=False), 0)
+    lax.fori_loop(0, steps, step, 0)
+
+    @pl.when(helper)
+    def _():
+        acc[:four] += guest_acc[:four]
+        acc[four:] += guest_acc[2 * four :]
 
     outbox[0] = fold(acc[:four], acc[four:])
 
@@ -427,9 +463,9 @@
         weights_to_helper().wait_recv()
         guest_both = stack(*split(guest_weights[1]))
 
-        def serve(c, _):
-            guest_out[:, span(c)] = means(guest_both, c)
-            mean_to_end(c).start()
+        def serve(g, _):
+            guest_out[:, span(g)] = means(guest_both, THIRD * g + 1)
+            mean_to_end(g).start()
             return 0
 
         lax.fori_loop(0, GUEST, serve, 0)
@@ -443,56 +479,54 @@
 
     def finish(c, _):
         at = span(c)
-        result_v[:, at] = base_v[:, at] + means(both, c)
-        store(c).start()
+
+        @pl.when(jnp.logical_not(end & left_out(c)))
+        def _():
+            result_v[:, at] = base_v[:, at] + means(both, c)
+            store(c).start()
+
         return 0
 
-    def finish_held(c, _):
-        at = span(c)
-        mean_to_end(c, -1).wait_recv()
-        result_v[:, at] = base_v[:, at] + guest_mean[:, at]
-        store(c).start()
-        return 0
-
-    lax.fori_loop(GUEST, CHUNKS, finish, 0)
+    lax.fori_loop(0, CHUNKS, finish, 0)
 
     @pl.when(end)
     def _():
-        lax.fori_loop(0, GUEST, finish_held, 0)
-        to_helper(0).wait_send()
-        to_helper(1).wait_send()
+        def receive(g, _):
+            c = THIRD * g + 1
+            mean_to_end(g, -1).wait_recv()
+            result_v[:, span(c)] = base_v[:, span(c)] + guest_mean[:, span(g)]
+            store(c).start()
+            to_helper(0, g).wait_send()
+            to_helper(1, g).wait_send()
+            return 0
+
+        lax.fori_loop(0, GUEST, receive, 0)
         weights_to_helper().wait_send()
 
-    @pl.when(jnp.logical_not(end))
-    def _():
-        lax.fori_loop(0, GUEST, finish, 0)
-
     @pl.when(helper)
     def _():
+        def sent(g, _):
+            mean_to_end(g).wait_send()
+            return 0
+
+        lax.fori_loop(0, GUEST, sent, 0)
         part_to_end().wait_send()
 
-    def drain(c, _, c_held):
+    def drain(c, _):
         store(c).wait()
         for origin in range(groups):
 
-            @pl.when((origin <= me) & goes(0, c_held))
+            @pl.when((origin <= me) & goes(0, c))
             def _(origin=origin):
                 hop(0, origin, c).wait_send()
 
-            @pl.when((origin >= me) & goes(1, c_held))
+            @pl.when((origin >= me) & goes(1, c))
             def _(origin=origin):
                 hop(1, origin, c).wait_send()
 
-        if c_held:
-
-            @pl.when(helper)
-            def _():
-                mean_to_end(c).wait_send()
-
         return 0
 
-    lax.fori_loop(0, GUEST, functools.partial(drain, c_held=True), 0)
-    lax.fori_loop(GUEST, CHUNKS, functools.partial(drain, c_held=False), 0)
+    lax.fori_loop(0, CHUNKS, drain, 0)
 
 
 def per_device(prior, samples, noise, obs_cells, obs_values, seismic_mask):
@@ -503,13 +537,17 @@
     rounds = shards.bit_length() - 1
     half = (2 * rows + ens) // 2
     held = GUEST * (cells // CHUNKS)
-    hbm = pl.BlockSpec(memory_space=pl.ANY)
+    hbm = pl.BlockSpec(memory_space=pltpu.HBM)
     f32 = jnp.float32
+    operands = [
+        pltpu.with_memory_space_constraint(x, pltpu.HBM)
+        for x in (prior, samples, noise, obs_cells, obs_values, seismic_mask)
+    ]
     return pl.pallas_call(
         functools.partial(kernel, groups, shards),
         out_shape=jax.ShapeDtypeStruct((rows, cells), f32),
         in_specs=[hbm] * 6,
-        out_specs=hbm,
+        out_specs=pl.BlockSpec(memory_space=pl.ANY),
         scratch_shapes=[
             pltpu.VMEM(obs_cells.shape, jnp.int32),
             pltpu.VMEM(obs_values.shape, f32),
@@ -539,15 +577,17 @@
             pltpu.VMEM((8 * rows + 2 * ens, 2 * ens), f32),
             pltpu.VMEM((2, half, 2 * ens), f32),
             pltpu.VMEM((2, 2 * rows, 2 * ens), f32),
-            pltpu.SemaphoreType.DMA((4,)),
-            pltpu.SemaphoreType.DMA((4,)),
+            pltpu.SemaphoreType.DMA((2, GUEST)),
+            pltpu.SemaphoreType.DMA((2, GUEST)),
+            pltpu.SemaphoreType.DMA((2,)),
+            pltpu.SemaphoreType.DMA((2,)),
             pltpu.SemaphoreType.DMA((GUEST,)),
             pltpu.SemaphoreType.DMA((GUEST,)),
         ],
         compiler_params=pltpu.CompilerParams(
-            collective_id=0, has_side_effects=True, vmem_limit_bytes=60 * 1024 * 1024
+            collective_id=0, has_side_effects=True, vmem_limit_bytes=48 * 1024 * 1024
         ),
-    )(prior, samples, noise, obs_cells, obs_values, seismic_mask)
+    )(*operands)
 
 
 def solution(mesh):

time: 84.1 us -> 79.8 us (0.949)
  Pallas kernels: 81.7 us -> 78.7 us
  local copies, waits for them, and re-layouts: 2.26 us -> 0.97 us
    pallas_call x1, Pallas kernels: 81.7 us -> 78.7 us  [per_device(): pl.pallas_call(functools.partial(kernel, groups, shards), out_shape=jax.S...]
    unnamed x1, local copies, waits for them, and re-layouts: 2.26 us -> 0.97 us
where the time goes in v3:
time: 79.8 us; the launch traced here: 79.6 us
  Pallas kernels  78.7 us (99%)
  local copies, waits for them, and re-layouts  0.97 us (1%)
    pallas_call x1, Pallas kernels, per_device(): pl.pallas_call(functools.partial(kernel, groups, shards), out_shape=jax.S...  78.7 us

profile of v3, /device:TPU:0, one launch (start us, length us, event | category | flops | bytes accessed | tf_op | source)
XLA Modules:
  0.0 79.6 jit_solution(1406539179890624081)
XLA Ops:
  0.0 78.7 %shard_map.64 = f32[16,16384]{1,0:T(8,128)S(1)} custom-call(f32[16,16384]{1,0:T(8,128)} %prior_ref.1, f32[16,16384]{1,0:T(8,128)} %samples_ref.1, f32[2,16,16384]{2,1,0:T(8,128)} %noise_ref.1, s32[2,2048]{1,0:T(2,128)} %cells_ref.1, f32[2,2048]{1,0:T(2,128)} %values_ref.1, s32[2,128]{1,0:T(2,128)} %mask_ref.1), custom_call_target="tpu_custom_call" | custom-call | tf_op jit(solution)/shard_map/pallas_call | solution.py:546
  78.7 1.0 %copy.8 = f32[16,16384]{1,0:T(8,128)} copy(f32[16,16384]{1,0:T(8,128)S(1)} %shard_map.64) | data formatting | bytes 2097152

commit v4 on v3

--- a/solution.py
+++ b/solution.py
@@ -14,7 +14,7 @@
 THIRD = 3
 GUEST = CHUNKS // THIRD
 LAG = 2
-AHEAD = 8
+AHEAD = 10
 OBS_CHUNK = 512
 MESH = pl.DeviceIdType.MESH
 NT = (((1,), (1,)), ((), ()))
@@ -95,7 +95,7 @@
     ens = rows * groups
     width = cells // CHUNKS
     ncell = cells * shards
-    rounds = shards.bit_length() - 1
+    peers = shards - 1
     low = 1 - (2 * me) // groups
     end = (me == 0) | (me == groups - 1)
     helper = (me == 1) | (me == groups - 2)
@@ -162,9 +162,15 @@
             device_id_type=MESH,
         )
 
-    def partner(r):
-        bit = 1 << r
-        return shard + bit * (1 - 2 * ((shard // bit) % 2))
+    def to_peer(k):
+        return pltpu.make_async_remote_copy(
+            src_ref=outbox,
+            dst_ref=inbox.at[k],
+            send_sem=red_send.at[k],
+            recv_sem=red_recv.at[k],
+            device_id={"cell": (shard + k + 1) % shards},
+            device_id_type=MESH,
+        )
 
     loads = [
         pltpu.make_async_copy(prior_ref, gath.at[me], local_sem.at[0]),
@@ -187,17 +193,19 @@
     def _():
         pl.semaphore_signal(barrier, inc=1, device_id={"member": me + 1}, device_id_type=MESH)
 
-    for r in range(rounds):
-        pl.semaphore_signal(barrier, inc=1, device_id={"cell": partner(r)}, device_id_type=MESH)
+    for k in range(peers):
+        pl.semaphore_signal(
+            barrier, inc=1, device_id={"cell": (shard + k + 1) % shards}, device_id_type=MESH
+        )
     inner = (me > 0) & (me < groups - 1)
 
     @pl.when(inner)
     def _():
-        pl.semaphore_wait(barrier, rounds + 2)
+        pl.semaphore_wait(barrier, peers + 2)
 
     @pl.when(jnp.logical_not(inner))
     def _():
-        pl.semaphore_wait(barrier, rounds + 1)
+        pl.semaphore_wait(barrier, peers + 1)
 
     def goes(way, c):
         if way == 0:
@@ -314,7 +322,6 @@
 
         lax.fori_loop(0, width // LANES, one, 0)
 
-    lax.fori_loop(0, blocks, prepare, 0)
     loads[0].wait()
     acc[...] = jnp.zeros_like(acc)
     guest_acc[...] = jnp.zeros_like(guest_acc)
@@ -371,6 +378,11 @@
             def _(c=c, d=d):
                 relay(c, d)
 
+        @pl.when(t < CHUNKS)
+        def _():
+            per = width // LANES
+            lax.fori_loop(t * per, t * per + per, prepare, 0)
+
         c = t - LAG * furthest
 
         @pl.when((c >= 0) & (c < CHUNKS))
@@ -400,28 +412,19 @@
         acc[:four] += guest_acc[:four]
         acc[four:] += guest_acc[2 * four :]
 
-    outbox[0] = fold(acc[:four], acc[four:])
+    outbox[...] = fold(acc[:four], acc[four:])
 
     @pl.when(end)
     def _():
         part_to_end(-1).wait_recv()
-        outbox[0] += guest_part[1]
-
-    part = outbox[0]
-    for r in range(rounds):
-        if r > 0:
-            outbox[r] = part
-        swap = pltpu.make_async_remote_copy(
-            src_ref=outbox.at[r],
-            dst_ref=inbox.at[r],
-            send_sem=red_send.at[r],
-            recv_sem=red_recv.at[r],
-            device_id={"cell": partner(r)},
-            device_id_type=MESH,
-        )
-        swap.start()
-        swap.wait()
-        part = part + inbox[r]
+        outbox[...] += guest_part[1]
+
+    for k in range(peers):
+        to_peer(k).start()
+    part = outbox[...]
+    for k in range(peers):
+        to_peer(k).wait_recv()
+        part = part + inbox[k]
     part = jnp.concatenate([part[:, :ens], part[:, ens:]], axis=0)
     cross0 = part[:rows]
     cross1 = part[rows : 2 * rows]
@@ -527,6 +530,8 @@
         return 0
 
     lax.fori_loop(0, CHUNKS, drain, 0)
+    for k in range(peers):
+        to_peer(k).wait_send()
 
 
 def per_device(prior, samples, noise, obs_cells, obs_values, seismic_mask):
@@ -534,7 +539,7 @@
     groups = lax.axis_size("member")
     shards = lax.axis_size("cell")
     ens = rows * groups
-    rounds = shards.bit_length() - 1
+    peers = shards - 1
     half = (2 * rows + ens) // 2
     held = GUEST * (cells // CHUNKS)
     hbm = pl.BlockSpec(memory_space=pltpu.HBM)
@@ -562,14 +567,14 @@
             pltpu.VMEM((rows, cells), f32),
             pltpu.VMEM((2, cells // LANES, LANES), f32),
             pltpu.VMEM((4 * rows + 2 * ens, 2 * ens), f32),
-            pltpu.VMEM((rounds, half, 2 * ens), f32),
-            pltpu.VMEM((rounds, half, 2 * ens), f32),
+            pltpu.VMEM((peers, half, 2 * ens), f32),
+            pltpu.VMEM((half, 2 * ens), f32),
             pltpu.SemaphoreType.DMA((6,)),
             pltpu.SemaphoreType.DMA((CHUNKS,)),
             pltpu.SemaphoreType.DMA((2, groups, CHUNKS)),
             pltpu.SemaphoreType.DMA((groups, CHUNKS)),
-            pltpu.SemaphoreType.DMA((rounds,)),
-            pltpu.SemaphoreType.DMA((rounds,)),
+            pltpu.SemaphoreType.DMA((peers,)),
+            pltpu.SemaphoreType.DMA((peers,)),
             pltpu.VMEM((2, rows, held), f32),
             pltpu.VMEM((4 * rows, held), jnp.bfloat16),
             pltpu.VMEM((rows, held), f32),

time: 79.8 us -> 79.5 us (level)
  no operation moved by 1% of the time
where the time goes in v4:
time: 79.5 us; the launch traced here: 79.4 us
  Pallas kernels  78.4 us (99%)
  local copies, waits for them, and re-layouts  0.97 us (1%)
    pallas_call x1, Pallas kernels, per_device(): pl.pallas_call(functools.partial(kernel, groups, shards), out_shape=jax.S...  78.4 us

profile of v4, /device:TPU:0, one launch (start us, length us, event | category | flops | bytes accessed | tf_op | source)
XLA Modules:
  0.0 79.4 jit_solution(17991991776419915666)
XLA Ops:
  0.0 78.4 %shard_map.64 = f32[16,16384]{1,0:T(8,128)S(1)} custom-call(f32[16,16384]{1,0:T(8,128)} %prior_ref.1, f32[16,16384]{1,0:T(8,128)} %samples_ref.1, f32[2,16,16384]{2,1,0:T(8,128)} %noise_ref.1, s32[2,2048]{1,0:T(2,128)} %cells_ref.1, f32[2,2048]{1,0:T(2,128)} %values_ref.1, s32[2,128]{1,0:T(2,128)} %mask_ref.1), custom_call_target="tpu_custom_call" | custom-call | tf_op jit(solution)/shard_map/pallas_call | solution.py:551
  78.4 1.0 %copy.8 = f32[16,16384]{1,0:T(8,128)} copy(f32[16,16384]{1,0:T(8,128)S(1)} %shard_map.64) | data formatting | bytes 2097152

commit v5 on v4

--- a/solution.py
+++ b/solution.py
@@ -13,6 +13,7 @@
 CHUNKS = 16
 THIRD = 3
 GUEST = CHUNKS // THIRD
+SERVED = GUEST - 2
 LAG = 2
 AHEAD = 10
 OBS_CHUNK = 512
@@ -104,7 +105,7 @@
     steps = CHUNKS + LAG * (groups - 1)
 
     def span(c):
-        return pl.ds(pl.multiple_of(c * width, width), width)
+        return pl.ds(c * width if isinstance(c, int) else pl.multiple_of(c * width, width), width)
 
     def hop(way, origin, c, own=False):
         target = me + 1 if way == 0 else me - 1
@@ -407,6 +408,20 @@
 
     lax.fori_loop(0, steps, step, 0)
 
+    late = [THIRD * g + 1 for g in range(SERVED, GUEST)]
+
+    @pl.when(me == 1)
+    def _():
+        for c in late:
+            for origin in range(1, groups):
+                hop(1, origin, c).start()
+
+    @pl.when(me == groups - 2)
+    def _():
+        for c in late:
+            for origin in range(groups - 1):
+                hop(0, origin, c).start()
+
     @pl.when(helper)
     def _():
         acc[:four] += guest_acc[:four]
@@ -471,7 +486,7 @@
             mean_to_end(g).start()
             return 0
 
-        lax.fori_loop(0, GUEST, serve, 0)
+        lax.fori_loop(0, SERVED, serve, 0)
 
     both = stack(*split(weights))
 
@@ -499,11 +514,32 @@
             mean_to_end(g, -1).wait_recv()
             result_v[:, span(c)] = base_v[:, span(c)] + guest_mean[:, span(g)]
             store(c).start()
+            return 0
+
+        def taken(g, _):
             to_helper(0, g).wait_send()
             to_helper(1, g).wait_send()
             return 0
 
-        lax.fori_loop(0, GUEST, receive, 0)
+        for c in late:
+
+            @pl.when(me == 0)
+            def _(c=c):
+                for origin in range(1, groups):
+                    hop(0, origin, c).wait_recv()
+
+            @pl.when(me == groups - 1)
+            def _(c=c):
+                for origin in range(groups - 1):
+                    hop(1, origin, c).wait_recv()
+
+            high, low = split(gath[:, :, span(c)].reshape(ens, width))
+            split_p[:ens, span(c)] = high
+            split_p[ens:, span(c)] = low
+            result_v[:, span(c)] = base_v[:, span(c)] + means(both, c)
+            store(c).start()
+        lax.fori_loop(0, SERVED, receive, 0)
+        lax.fori_loop(0, GUEST, taken, 0)
         weights_to_helper().wait_send()
 
     @pl.when(helper)
@@ -512,7 +548,7 @@
             mean_to_end(g).wait_send()
             return 0
 
-        lax.fori_loop(0, GUEST, sent, 0)
+        lax.fori_loop(0, SERVED, sent, 0)
         part_to_end().wait_send()
 
     def drain(c, _):
@@ -530,6 +566,19 @@
         return 0
 
     lax.fori_loop(0, CHUNKS, drain, 0)
+
+    @pl.when(me == 1)
+    def _():
+        for c in late:
+            for origin in range(1, groups):
+                hop(1, origin, c).wait_send()
+
+    @pl.when(me == groups - 2)
+    def _():
+        for c in late:
+            for origin in range(groups - 1):
+                hop(0, origin, c).wait_send()
+
     for k in range(peers):
         to_peer(k).wait_send()
 

time: 79.5 us -> 78.3 us (0.985)
  Pallas kernels: 78.4 us -> 77.2 us
    pallas_call x1, Pallas kernels: 78.4 us -> 77.2 us  [per_device(): pl.pallas_call(functools.partial(kernel, groups, shards), out_shape=jax.S...]
where the time goes in v5:
time: 78.3 us; the launch traced here: 78.2 us
  Pallas kernels  77.2 us (99%)
  local copies, waits for them, and re-layouts  0.97 us (1%)
    pallas_call x1, Pallas kernels, per_device(): pl.pallas_call(functools.partial(kernel, groups, shards), out_shape=jax.S...  77.2 us

profile of v5, /device:TPU:0, one launch (start us, length us, event | category | flops | bytes accessed | tf_op | source)
XLA Modules:
  0.0 78.2 jit_solution(6057717199753448216)
XLA Ops:
  0.0 77.2 %shard_map.64 = f32[16,16384]{1,0:T(8,128)S(1)} custom-call(f32[16,16384]{1,0:T(8,128)} %prior_ref.1, f32[16,16384]{1,0:T(8,128)} %samples_ref.1, f32[2,16,16384]{2,1,0:T(8,128)} %noise_ref.1, s32[2,2048]{1,0:T(2,128)} %cells_ref.1, f32[2,2048]{1,0:T(2,128)} %values_ref.1, s32[2,128]{1,0:T(2,128)} %mask_ref.1), custom_call_target="tpu_custom_call" | custom-call | tf_op jit(solution)/shard_map/pallas_call | solution.py:600
  77.2 1.0 %copy.8 = f32[16,16384]{1,0:T(8,128)} copy(f32[16,16384]{1,0:T(8,128)S(1)} %shard_map.64) | data formatting | bytes 2097152

commit v6 on v5

--- a/solution.py
+++ b/solution.py
@@ -507,6 +507,34 @@
 
     lax.fori_loop(0, CHUNKS, finish, 0)
 
+    def drain(c, _):
+        for origin in range(groups):
+
+            @pl.when((origin <= me) & goes(0, c))
+            def _(origin=origin):
+                hop(0, origin, c).wait_send()
+
+            @pl.when((origin >= me) & goes(1, c))
+            def _(origin=origin):
+                hop(1, origin, c).wait_send()
+
+        return 0
+
+    lax.fori_loop(0, CHUNKS, drain, 0)
+    for k in range(peers):
+        to_peer(k).wait_send()
+
+    @pl.when(end)
+    def _():
+        def taken(g, _):
+            to_helper(0, g).wait_send()
+            to_helper(1, g).wait_send()
+            return 0
+
+        lax.fori_loop(0, GUEST, taken, 0)
+        weights_to_helper().wait_send()
+
+
     @pl.when(end)
     def _():
         def receive(g, _):
@@ -516,11 +544,6 @@
             store(c).start()
             return 0
 
-        def taken(g, _):
-            to_helper(0, g).wait_send()
-            to_helper(1, g).wait_send()
-            return 0
-
         for c in late:
 
             @pl.when(me == 0)
@@ -539,8 +562,6 @@
             result_v[:, span(c)] = base_v[:, span(c)] + means(both, c)
             store(c).start()
         lax.fori_loop(0, SERVED, receive, 0)
-        lax.fori_loop(0, GUEST, taken, 0)
-        weights_to_helper().wait_send()
 
     @pl.when(helper)
     def _():
@@ -551,21 +572,11 @@
         lax.fori_loop(0, SERVED, sent, 0)
         part_to_end().wait_send()
 
-    def drain(c, _):
+    def written(c, _):
         store(c).wait()
-        for origin in range(groups):
-
-            @pl.when((origin <= me) & goes(0, c))
-            def _(origin=origin):
-                hop(0, origin, c).wait_send()
-
-            @pl.when((origin >= me) & goes(1, c))
-            def _(origin=origin):
-                hop(1, origin, c).wait_send()
-
         return 0
 
-    lax.fori_loop(0, CHUNKS, drain, 0)
+    lax.fori_loop(0, CHUNKS, written, 0)
 
     @pl.when(me == 1)
     def _():
@@ -578,9 +589,6 @@
         for c in late:
             for origin in range(groups - 1):
                 hop(0, origin, c).wait_send()
-
-    for k in range(peers):
-        to_peer(k).wait_send()
 
 
 def per_device(prior, samples, noise, obs_cells, obs_values, seismic_mask):

time: 78.3 us -> 77.9 us (level)
  no operation moved by 1% of the time
where the time goes in v6:
time: 77.9 us; the launch traced here: 77.7 us
  Pallas kernels  76.7 us (98%)
  local copies, waits for them, and re-layouts  0.97 us (1%)
    pallas_call x1, Pallas kernels, per_device(): pl.pallas_call(functools.partial(kernel, groups, shards), out_shape=jax.S...  76.7 us

profile of v6, /device:TPU:0, one launch (start us, length us, event | category | flops | bytes accessed | tf_op | source)
XLA Modules:
  0.0 77.7 jit_solution(1107557193361666673)
XLA Ops:
  0.0 76.7 %shard_map.64 = f32[16,16384]{1,0:T(8,128)S(1)} custom-call(f32[16,16384]{1,0:T(8,128)} %prior_ref.1, f32[16,16384]{1,0:T(8,128)} %samples_ref.1, f32[2,16,16384]{2,1,0:T(8,128)} %noise_ref.1, s32[2,2048]{1,0:T(2,128)} %cells_ref.1, f32[2,2048]{1,0:T(2,128)} %values_ref.1, s32[2,128]{1,0:T(2,128)} %mask_ref.1), custom_call_target="tpu_custom_call" | custom-call | tf_op jit(solution)/shard_map/pallas_call | solution.py:608
  76.7 1.0 %copy.8 = f32[16,16384]{1,0:T(8,128)} copy(f32[16,16384]{1,0:T(8,128)S(1)} %shard_map.64) | data formatting | bytes 2097152

commit v7 on v6

--- a/solution.py
+++ b/solution.py
@@ -15,7 +15,7 @@
 GUEST = CHUNKS // THIRD
 SERVED = GUEST - 2
 LAG = 2
-AHEAD = 10
+AHEAD = 14
 OBS_CHUNK = 512
 MESH = pl.DeviceIdType.MESH
 NT = (((1,), (1,)), ((), ()))

time: 77.9 us -> 79.3 us (1.018)
  Pallas kernels: 76.7 us -> 78.1 us
    pallas_call x1, Pallas kernels: 76.7 us -> 78.1 us  [per_device(): pl.pallas_call(functools.partial(kernel, groups, shards), out_shape=jax.S...]
where the time goes in v7:
time: 79.3 us; the launch traced here: 79.1 us
  Pallas kernels  78.1 us (98%)
  local copies, waits for them, and re-layouts  0.97 us (1%)
    pallas_call x1, Pallas kernels, per_device(): pl.pallas_call(functools.partial(kernel, groups, shards), out_shape=jax.S...  78.1 us

profile of v7, /device:TPU:0, one launch (start us, length us, event | category | flops | bytes accessed | tf_op | source)
XLA Modules:
  0.0 79.1 jit_solution(5119340249227169699)
XLA Ops:
  0.0 78.1 %shard_map.64 = f32[16,16384]{1,0:T(8,128)S(1)} custom-call(f32[16,16384]{1,0:T(8,128)} %prior_ref.1, f32[16,16384]{1,0:T(8,128)} %samples_ref.1, f32[2,16,16384]{2,1,0:T(8,128)} %noise_ref.1, s32[2,2048]{1,0:T(2,128)} %cells_ref.1, f32[2,2048]{1,0:T(2,128)} %values_ref.1, s32[2,128]{1,0:T(2,128)} %mask_ref.1), custom_call_target="tpu_custom_call" | custom-call | tf_op jit(solution)/shard_map/pallas_call | solution.py:608
  78.1 1.0 %copy.8 = f32[16,16384]{1,0:T(8,128)} copy(f32[16,16384]{1,0:T(8,128)S(1)} %shard_map.64) | data formatting | bytes 2097152
